TPU v7x, 32 devices: a whole 2x2x4 slice. The times are simulated.
32 devices in a mesh: seq: 16 (over z, y, core), head: 2 (over x), dp: 1.
Axes of the slice: x: 2, y: 2, z: 4, core: 2. Of those that a mesh axis runs over, the one named last changes fastest.
Arguments:
- queries: bfloat16 [4096, 2048], P(('dp', 'seq', 'head')), may hold values from -9 to 9
- keys: bfloat16 [4096, 2048], P(('dp', 'seq', 'head')), may hold values from -9 to 9
- values: bfloat16 [4096, 2048], P(('dp', 'seq', 'head')), may hold values from -6 to 6
- coords: int32 [3, 4096], P(None, ('dp', 'seq', 'head')), may hold values from 0 to 511, as said below
- lengths: int32 [32], P('dp'), may hold values from 1 to 384, 4096 in all
Outputs:
- attention: bfloat16 [4096, 2048], P(('dp', 'seq', 'head'))
Inputs may be any that keep to these rules, and one draw needn't show every extreme that they name: `coords`: voxel coordinates of each token along x, y and z. `lengths`: the token counts of the 32 scenes of a pack in order; they sum to 4096 and the longest scene has exactly 384 tokens.
All inputs are finite; a program needn't handle non-finite values.
Results may differ from a plain program's by a relative error of at most 0.012.
Values may be sent and summed in bfloat16 or wider, within the bound.
A program may use at most 128 MiB of HBM per device.

v0:
```python
import functools

import jax
import jax.numpy as jnp
import numpy as np
from jax import lax
from jax.experimental import pallas as pl
from jax.experimental.pallas import tpu as pltpu
from jax.sharding import PartitionSpec as P

HD = 64
GROUP_DEVICES = 8
NEG_BIG = -1e30
SCORE_SCALE = 0.125


def frequency_rows():
    pair_count = HD // 2
    pair = np.arange(pair_count)
    exponent = (3 * pair % pair_count) / pair_count
    column = (100.0 ** -exponent).astype(np.float32)
    return np.tile(column[:, None], (1, 128))


def attention_kernel(
    sizes,
    q_hbm, k_hbm, v_hbm, coords_ref, lengths_ref, freq_ref,
    out_ref,
    q_in, k_in, q_rot, k_rot, q_buf, k_buf, v_buf, o_buf, key_scene, query_scene,
    in_sem, q_send, q_recv, kv_send, kv_recv, halo_send, o_send, o_recv, own_sem,
):
    head_count, members, groups, rows, cols, reach_blocks, scenes = sizes
    heads = cols // HD
    spans = -(-reach_blocks // members)
    blocks = members + 2 * reach_blocks
    window = (2 * reach_blocks + 1) * rows
    flat = lax.axis_index("seq") * head_count + lax.axis_index("head")
    group = flat // members
    me = flat % members

    def device(group_at, member_at):
        at = group_at * members + member_at
        return {"seq": at // head_count, "head": at % head_count}

    def columns(member_at):
        return pl.ds(pl.multiple_of(member_at * cols, cols), cols)

    def block(index):
        return pl.ds(pl.multiple_of(index * rows, rows), rows)

    shifts = [e for d in range(1, spans + 1) for e in (d, -d)]

    load_k = pltpu.make_async_copy(k_hbm, k_in, in_sem.at[0])
    load_q = pltpu.make_async_copy(q_hbm, q_in, in_sem.at[1])
    load_k.start()
    load_q.start()
    own_v = pltpu.make_async_copy(
        v_hbm.at[:, columns(me)], v_buf.at[block(reach_blocks + me)], own_sem.at[0]
    )
    own_v.start()

    barrier = pltpu.get_barrier_semaphore()
    for i in range(1, members):
        pl.semaphore_signal(barrier, inc=1, device_id=device(group, (me + i) % members))
    expected = members - 1
    for e in shifts:
        there = (group + e >= 0) & (group + e < groups)

        @pl.when(there)
        def _():
            pl.semaphore_signal(barrier, inc=1, device_id=device(group + e, me))

        expected = expected + there.astype(jnp.int32)
    pl.semaphore_wait(barrier, expected)

    bufs = (v_buf, k_buf)

    def kv_copy(which, source, i, other, index):
        return pltpu.make_async_remote_copy(
            src_ref=source,
            dst_ref=bufs[which].at[block(index)],
            send_sem=kv_send.at[which, i],
            recv_sem=kv_recv.at[which, index],
            device_id=device(group, other),
        )

    v_copies = []
    for i in range(1, members):
        other = (me + i) % members
        copy = kv_copy(0, v_hbm.at[:, columns(other)], i, other, reach_blocks + me)
        copy.start()
        v_copies.append(copy)

    pair = lax.broadcasted_iota(jnp.int32, (HD // 2, rows), 0)
    axis_of = 3 * pair // (HD // 2)
    position = jnp.where(
        axis_of == 0,
        coords_ref[0:1, :],
        jnp.where(axis_of == 1, coords_ref[1:2, :], coords_ref[2:3, :]),
    ).astype(jnp.float32)
    angles = position * freq_ref[...]

    def spread(table):
        tall = jnp.concatenate([table] * (128 // (HD // 2)), axis=0).T
        return jnp.concatenate([tall] * (cols // 128), axis=1)

    cos_all = spread(jnp.cos(angles))
    sin_all = spread(jnp.sin(angles))
    from_row = lax.broadcasted_iota(jnp.int32, (cols, cols), 0)
    to_col = lax.broadcasted_iota(jnp.int32, (cols, cols), 1)
    front = to_col % HD < HD // 2
    swap = jnp.where(
        front & (from_row == to_col + HD // 2),
        -1.0,
        jnp.where((to_col % HD >= HD // 2) & (from_row == to_col - HD // 2), 1.0, 0.0),
    ).astype(jnp.bfloat16)

    def rotated(tile, scale):
        swapped = jnp.dot(tile, swap, preferred_element_type=jnp.float32)
        turned = tile.astype(jnp.float32) * cos_all + swapped * sin_all
        return (turned * scale).astype(jnp.bfloat16)

    load_k.wait()
    k_copies = []
    for i in range(1, members):
        other = (me + i) % members
        k_rot[i] = rotated(k_in[:, columns(other)], 1.0)
        copy = kv_copy(1, k_rot.at[i], i, other, reach_blocks + me)
        copy.start()
        k_copies.append(copy)
    k_buf[block(reach_blocks + me), :] = rotated(k_in[:, columns(me)], 1.0)

    load_q.wait()
    q_copies = []
    for i in range(1, members):
        other = (me + i) % members
        q_rot[i] = rotated(q_in[:, columns(other)], SCORE_SCALE)
        copy = pltpu.make_async_remote_copy(
            src_ref=q_rot.at[i],
            dst_ref=q_buf.at[block(me)],
            send_sem=q_send.at[i],
            recv_sem=q_recv.at[me],
            device_id=device(group, other),
        )
        copy.start()
        q_copies.append(copy)
    q_buf[block(me), :] = rotated(q_in[:, columns(me)], SCORE_SCALE)

    first = (group * members - reach_blocks) * rows
    token = first + lax.broadcasted_iota(jnp.int32, (8, blocks * rows), 1)
    scene = jnp.zeros((8, blocks * rows), jnp.int32)
    end = jnp.int32(0)
    for s in range(scenes):
        end = end + lengths_ref[s]
        scene = scene + (token >= end).astype(jnp.int32)
    key_scene[...] = jnp.where(token < 0, -1, scene).astype(jnp.float32)
    for b in range(members):
        row = key_scene[0:1, (reach_blocks + b) * rows : (reach_blocks + b + 1) * rows]
        query_scene[b] = jnp.broadcast_to(row, (128, rows)).T

    for e in shifts:
        held = [p for p in range(members) if 0 <= reach_blocks + p - e * members < blocks]
        low = (reach_blocks + held[0] - e * members) * rows
        high = (reach_blocks + held[-1] - e * members + 1) * rows

        @pl.when((group - e < 0) | (group - e >= groups))
        def _():
            for buf in bufs:
                buf[low:high, :] = jnp.zeros((high - low, cols), jnp.bfloat16)

    def halo_copy(which, p, e):
        index = reach_blocks + p - e * members
        return pltpu.make_async_remote_copy(
            src_ref=bufs[which].at[block(reach_blocks + p)],
            dst_ref=bufs[which].at[block(index)],
            send_sem=halo_send.at[which, shifts.index(e), p],
            recv_sem=kv_recv.at[which, index],
            device_id=device(group + e, me),
        )

    routes = [
        (p, [e for e in shifts if 0 <= reach_blocks + p - e * members < blocks])
        for p in range(members)
    ]
    routes.sort(key=lambda route: -len(route[1]))
    own_v.wait()
    for which in range(2):
        for p, goes in routes:

            @pl.when(me != p)
            def _():
                kv_copy(which, k_rot.at[0], 0, p, reach_blocks + p).wait_recv()

            for e in goes:

                @pl.when((group + e >= 0) & (group + e < groups))
                def _():
                    halo_copy(which, p, e).start()

    for which in range(2):
        for p, goes in routes:
            for e in goes:

                @pl.when((group - e >= 0) & (group - e < groups))
                def _():
                    halo_copy(which, p, e).wait_recv()

    for i in range(1, members):
        other = (me + i) % members
        pltpu.make_async_remote_copy(
            src_ref=q_rot.at[0],
            dst_ref=q_buf.at[block(other)],
            send_sem=q_send.at[0],
            recv_sem=q_recv.at[other],
            device_id=device(group, other),
        ).wait_recv()

    lane_head = lax.broadcasted_iota(jnp.int32, (rows, cols), 1) // HD

    def out_copy(i, other):
        return pltpu.make_async_remote_copy(
            src_ref=o_buf.at[i],
            dst_ref=out_ref.at[:, columns(me)],
            send_sem=o_send.at[i],
            recv_sem=o_recv.at[me],
            device_id=device(group, other),
        )

    def attend(i, carry):
        b = (me + i) % members
        q_tile = q_buf[block(b), :]
        span = pl.ds(pl.multiple_of(b * rows, rows), window)
        k_tile = k_buf[span, :]
        v_tile = v_buf[span, :]
        q_scene = jnp.concatenate([query_scene[b]] * (window // 128), axis=1)
        allowed = q_scene == key_scene[0:1, span]
        result = jnp.zeros((rows, cols), jnp.float32)
        for h in range(heads):
            q_one = jnp.where(lane_head == h, q_tile, jnp.bfloat16(0.0))
            scores = lax.dot_general(
                q_one, k_tile, (((1,), (1,)), ((), ())), preferred_element_type=jnp.float32
            )
            scores = jnp.where(allowed, scores, NEG_BIG)
            top = jnp.max(scores, axis=1, keepdims=True)
            weights = jnp.exp(scores - top)
            total = jnp.sum(weights, axis=1, keepdims=True)
            mixed = jnp.dot(
                weights.astype(jnp.bfloat16), v_tile, preferred_element_type=jnp.float32
            )
            result = jnp.where(lane_head == h, mixed / total, result)
        o_buf[i] = result.astype(jnp.bfloat16)
        return carry

    def attend_and_send(i, carry):
        attend(i, 0)
        out_copy(i, (me + i) % members).start()
        return carry

    lax.fori_loop(1, members, attend_and_send, 0)
    attend(0, 0)
    own_o = pltpu.make_async_copy(o_buf.at[0], out_ref.at[:, columns(me)], own_sem.at[1])
    own_o.start()

    for copy in v_copies + k_copies + q_copies:
        copy.wait_send()
    for which in range(2):
        for p, goes in routes:
            for e in goes:

                @pl.when((group + e >= 0) & (group + e < groups))
                def _():
                    halo_copy(which, p, e).wait_send()

    for i in range(1, members):
        out_copy(i, (me + i) % members).wait_send()
    for i in range(1, members):
        other = (me + i) % members
        pltpu.make_async_remote_copy(
            src_ref=o_buf.at[0],
            dst_ref=out_ref.at[:, columns(other)],
            send_sem=o_send.at[0],
            recv_sem=o_recv.at[other],
            device_id=device(group, other),
        ).wait_recv()
    own_o.wait()


def local(queries, keys, values, coords, lengths):
    rows, all_cols = queries.shape
    head_count = lax.axis_size("head")
    seq_count = lax.axis_size("seq")
    members = GROUP_DEVICES
    groups = seq_count * head_count // members
    cols = all_cols // members
    scenes = lengths.shape[0]
    total = rows * seq_count * head_count
    longest = 3 * total // scenes
    reach_blocks = -(-(longest - 1) // rows)
    blocks = members + 2 * reach_blocks
    spans = -(-reach_blocks // members)
    sizes = (head_count, members, groups, rows, cols, reach_blocks, scenes)
    window = (2 * reach_blocks + 1) * rows
    bf16, dma = jnp.bfloat16, pltpu.SemaphoreType.DMA
    anywhere = pl.BlockSpec(memory_space=pl.ANY)
    in_vmem = pl.BlockSpec(memory_space=pltpu.VMEM)
    return pl.pallas_call(
        functools.partial(attention_kernel, sizes),
        out_shape=jax.ShapeDtypeStruct((rows, all_cols), bf16),
        in_specs=[
            anywhere, anywhere, anywhere, in_vmem,
            pl.BlockSpec(memory_space=pltpu.SMEM), in_vmem,
        ],
        out_specs=anywhere,
        scratch_shapes=[
            pltpu.VMEM((rows, all_cols), bf16),
            pltpu.VMEM((rows, all_cols), bf16),
            pltpu.VMEM((members, rows, cols), bf16),
            pltpu.VMEM((members, rows, cols), bf16),
            pltpu.VMEM((members * rows, cols), bf16),
            pltpu.VMEM((blocks * rows, cols), bf16),
            pltpu.VMEM((blocks * rows, cols), bf16),
            pltpu.VMEM((members, rows, cols), bf16),
            pltpu.VMEM((8, blocks * rows), jnp.float32),
            pltpu.VMEM((members, rows, 128), jnp.float32),
            dma((2,)),
            dma((members,)),
            dma((members,)),
            dma((2, members)),
            dma((2, blocks)),
            dma((2, 2 * spans, members)),
            dma((members,)),
            dma((members,)),
            dma((2,)),
        ],
        compiler_params=pltpu.CompilerParams(
            collective_id=0, has_side_effects=True, vmem_limit_bytes=48 * 1024 * 1024
        ),
        cost_estimate=pl.CostEstimate(
            flops=4 * members * rows * window * cols,
            bytes_accessed=8 * rows * all_cols,
            transcendentals=members * rows * window * (cols // HD),
        ),
    )(queries, keys, values, coords, lengths, jnp.asarray(frequency_rows()))


def solution(mesh):
    in_specs = (
        P(("dp", "seq", "head"), None),
        P(("dp", "seq", "head"), None),
        P(("dp", "seq", "head"), None),
        P(None, ("dp", "seq", "head")),
        P("dp"),
    )
    out_specs = P(("dp", "seq", "head"), None)
    return jax.shard_map(local, mesh=mesh, in_specs=in_specs, out_specs=out_specs, check_vma=False)
```

profile of v0, /device:TPU:0, one launch (start us, length us, event | category | flops | bytes accessed | tf_op | source)
XLA Modules:
  0.0 46.9 jit_solution(3313545079234503900)
XLA Ops:
  0.0 0.0 copy-start
  0.0 1.0 %copy-done = bf16[128,2048]{1,0:T(8,128)(2,1)S(1)} copy-done((bf16[128,2048]{1,0:T(8,128)(2,1)S(1)}, bf16[128,2048]{1,0:T(8,128)(2,1)}, u32[]{:S(2)}) %copy-start) | copy-done | bytes 524312
  1.0 0.0 copy-start.1
  1.0 1.0 %copy-done.1 = bf16[128,2048]{1,0:T(8,128)(2,1)S(1)} copy-done((bf16[128,2048]{1,0:T(8,128)(2,1)S(1)}, bf16[128,2048]{1,0:T(8,128)(2,1)}, u32[]{:S(2)}) %copy-start.1) | copy-done | bytes 524312
  2.1 0.0 copy-start.2
  2.1 1.0 %copy-done.2 = bf16[128,2048]{1,0:T(8,128)(2,1)S(1)} copy-done((bf16[128,2048]{1,0:T(8,128)(2,1)S(1)}, bf16[128,2048]{1,0:T(8,128)(2,1)}, u32[]{:S(2)}) %copy-start.2) | copy-done | bytes 524312
  3.1 0.0 copy-start.3
  3.1 0.7 %copy-done.3 = s32[3,128]{1,0:T(4,128)S(1)} copy-done((s32[3,128]{1,0:T(4,128)S(1)}, s32[3,128]{1,0:T(4,128)}, u32[]{:S(2)}) %copy-start.3) | copy-done | bytes 1560
  3.8 0.0 copy-start.4
  3.8 0.7 %copy-done.4 = s32[32]{0:T(128)S(1)} copy-done((s32[32]{0:T(128)S(1)}, s32[32]{0:T(128)}, u32[]{:S(2)}) %copy-start.4) | copy-done | bytes 152
  4.5 0.0 copy-start.5
  4.5 0.7 %copy-done.5 = f32[32,128]{1,0:T(8,128)S(1)} copy-done((f32[32,128]{1,0:T(8,128)S(1)}, f32[32,128]{1,0:T(8,128)}, u32[]{:S(2)}) %copy-start.5) | copy-done | bytes 16408
  5.2 40.9 %shard_map.64 = bf16[128,2048]{1,0:T(8,128)(2,1)S(1)} custom-call(bf16[128,2048]{1,0:T(8,128)(2,1)S(1)} %copy-done, bf16[128,2048]{1,0:T(8,128)(2,1)S(1)} %copy-done.1, bf16[128,2048]{1,0:T(8,128)(2,1)S(1)} %copy-done.2, s32[3,128]{1,0:T(4,128)S(1)} %copy-done.3, s32[32]{0:T(128)S(1)} %copy-done.4, f32[32,128]{1,0:T(8,128)S(1)} %copy-done.5), custom_call_target="tpu_custom_call" | custom-call | flops 939524096 | bytes 2097152 | tf_op jit(solution)/shard_map/pallas_call | solution.py:306
  46.1 0.8 %copy.8 = bf16[128,2048]{1,0:T(8,128)(2,1)} copy(bf16[128,2048]{1,0:T(8,128)(2,1)S(1)} %shard_map.64) | data formatting | bytes 1048576
Async XLA Ops:
  0.0 1.0 %copy-start = (bf16[128,2048]{1,0:T(8,128)(2,1)S(1)}, bf16[128,2048]{1,0:T(8,128)(2,1)}, u32[]{:S(2)}) copy-start(bf16[128,2048]{1,0:T(8,128)(2,1)} %q_hbm.1) | copy-start | bytes 1572868
  1.0 1.0 %copy-start.1 = (bf16[128,2048]{1,0:T(8,128)(2,1)S(1)}, bf16[128,2048]{1,0:T(8,128)(2,1)}, u32[]{:S(2)}) copy-start(bf16[128,2048]{1,0:T(8,128)(2,1)} %k_hbm.1) | copy-start | bytes 1572868
  2.1 1.0 %copy-start.2 = (bf16[128,2048]{1,0:T(8,128)(2,1)S(1)}, bf16[128,2048]{1,0:T(8,128)(2,1)}, u32[]{:S(2)}) copy-start(bf16[128,2048]{1,0:T(8,128)(2,1)} %v_hbm.1) | copy-start | bytes 1572868
  3.1 0.7 %copy-start.3 = (s32[3,128]{1,0:T(4,128)S(1)}, s32[3,128]{1,0:T(4,128)}, u32[]{:S(2)}) copy-start(s32[3,128]{1,0:T(4,128)} %coords_ref.1) | copy-start | bytes 4612
  3.8 0.7 %copy-start.4 = (s32[32]{0:T(128)S(1)}, s32[32]{0:T(128)}, u32[]{:S(2)}) copy-start(s32[32]{0:T(128)} %lengths_ref.1) | copy-start | bytes 388
  4.5 0.7 %copy-start.5 = (f32[32,128]{1,0:T(8,128)S(1)}, f32[32,128]{1,0:T(8,128)}, u32[]{:S(2)}) copy-start(f32[32,128]{1,0:T(8,128)} %constant.2.clone.freq_ref) | copy-start | bytes 49156
where the time goes:
time: 47.2 us; the launch traced here: 46.9 us
  Pallas kernels  40.9 us (87%)
  local copies, waits for them, and re-layouts  5.97 us (13%)
    pallas_call x1, Pallas kernels, local(): pl.pallas_call(functools.partial(attention_kernel, sizes), out_shape=jax....  40.9 us
    unnamed x13, local copies, waits for them, and re-layouts  5.97 us

commit v1 on v0

v1 whole, which is shorter than its diff:
```python
import functools

import jax
import jax.numpy as jnp
import numpy as np
from jax import lax
from jax.experimental import pallas as pl
from jax.experimental.pallas import tpu as pltpu
from jax.sharding import PartitionSpec as P

HD = 64
GROUP_DEVICES = 8
NEG_BIG = -1e30
SCORE_SCALE = 0.125


def frequencies():
    pair_count = HD // 2
    exponent = (3 * np.arange(pair_count) % pair_count) / pair_count
    return [float(f) for f in (100.0 ** -exponent).astype(np.float32)]


def attention_kernel(
    sizes,
    q_hbm, k_hbm, v_hbm, coords_hbm, lengths_hbm,
    out_ref,
    coords_ref, lengths_ref, q_in, k_in, q_rot, k_rot, q_buf, k_buf, v_buf, o_buf, key_scene, query_scene,
    in_sem, q_send, q_recv, kv_send, kv_recv, halo_send, o_send, o_recv, own_sem,
):
    head_count, members, groups, rows, cols, reach_blocks, scenes = sizes
    heads = cols // HD
    spans = -(-reach_blocks // members)
    blocks = members + 2 * reach_blocks
    window = (2 * reach_blocks + 1) * rows
    flat = lax.axis_index("seq") * head_count + lax.axis_index("head")
    group = flat // members
    me = flat % members

    def device(group_at, member_at):
        at = group_at * members + member_at
        return {"seq": at // head_count, "head": at % head_count}

    def columns(member_at):
        return pl.ds(pl.multiple_of(member_at * cols, cols), cols)

    def block(index):
        return pl.ds(pl.multiple_of(index * rows, rows), rows)

    shifts = [e for d in range(1, spans + 1) for e in (d, -d)]

    load_k = pltpu.make_async_copy(k_hbm, k_in, in_sem.at[0])
    load_q = pltpu.make_async_copy(q_hbm, q_in, in_sem.at[1])
    load_coords = pltpu.make_async_copy(coords_hbm, coords_ref, in_sem.at[2])
    load_lengths = pltpu.make_async_copy(lengths_hbm, lengths_ref, in_sem.at[3])
    load_coords.start()
    load_k.start()
    load_q.start()
    load_lengths.start()
    own_v = pltpu.make_async_copy(
        v_hbm.at[:, columns(me)], v_buf.at[reach_blocks + me], own_sem.at[0]
    )
    own_v.start()

    barrier = pltpu.get_barrier_semaphore()
    for i in range(1, members):
        pl.semaphore_signal(barrier, inc=1, device_id=device(group, (me + i) % members))
    expected = members - 1
    for e in shifts:
        there = (group + e >= 0) & (group + e < groups)

        @pl.when(there)
        def _():
            pl.semaphore_signal(barrier, inc=1, device_id=device(group + e, me))

        expected = expected + there.astype(jnp.int32)
    pl.semaphore_wait(barrier, expected)

    bufs = (v_buf, k_buf)

    def kv_copy(which, source, i, other, index):
        return pltpu.make_async_remote_copy(
            src_ref=source,
            dst_ref=bufs[which].at[index],
            send_sem=kv_send.at[which, i],
            recv_sem=kv_recv.at[which, index],
            device_id=device(group, other),
        )

    v_copies = []
    for i in range(1, members):
        other = (me + i) % members
        copy = kv_copy(0, v_hbm.at[:, columns(other)], i, other, reach_blocks + me)
        copy.start()
        v_copies.append(copy)

    pair = lax.broadcasted_iota(jnp.int32, (HD // 2, rows), 0)
    axis_of = 3 * pair // (HD // 2)
    load_coords.wait()
    position = jnp.where(
        axis_of == 0,
        coords_ref[0:1, :],
        jnp.where(axis_of == 1, coords_ref[1:2, :], coords_ref[2:3, :]),
    ).astype(jnp.float32)
    frequency = jnp.zeros((HD // 2, rows), jnp.float32)
    for p, value in enumerate(frequencies()):
        frequency = jnp.where(pair == p, value, frequency)
    angles = position * frequency

    def spread(table):
        tall = jnp.concatenate([table] * (128 // (HD // 2)), axis=0).T
        return jnp.concatenate([tall] * (cols // 128), axis=1)

    cos_all = spread(jnp.cos(angles))
    sin_all = spread(jnp.sin(angles))
    from_row = lax.broadcasted_iota(jnp.int32, (cols, cols), 0)
    to_col = lax.broadcasted_iota(jnp.int32, (cols, cols), 1)
    front = to_col % HD < HD // 2
    swap = jnp.where(
        front & (from_row == to_col + HD // 2),
        -1.0,
        jnp.where((to_col % HD >= HD // 2) & (from_row == to_col - HD // 2), 1.0, 0.0),
    ).astype(jnp.bfloat16)

    def rotated(tile, scale):
        swapped = jnp.dot(tile, swap, preferred_element_type=jnp.float32)
        turned = tile.astype(jnp.float32) * cos_all + swapped * sin_all
        return (turned * scale).astype(jnp.bfloat16)

    load_k.wait()
    k_copies = []
    for i in range(1, members):
        other = (me + i) % members
        k_rot[i] = rotated(k_in[:, columns(other)], 1.0).T
        copy = kv_copy(1, k_rot.at[i], i, other, reach_blocks + me)
        copy.start()
        k_copies.append(copy)
    k_buf[reach_blocks + me] = rotated(k_in[:, columns(me)], 1.0).T

    for e in shifts:
        held = [p for p in range(members) if 0 <= reach_blocks + p - e * members < blocks]
        low = reach_blocks + held[0] - e * members
        high = reach_blocks + held[-1] - e * members + 1

        @pl.when((group - e < 0) | (group - e >= groups))
        def _():
            for buf in bufs:
                buf[low:high] = jnp.zeros((high - low,) + buf.shape[1:], jnp.bfloat16)

    def halo_copy(which, p, e):
        index = reach_blocks + p - e * members
        return pltpu.make_async_remote_copy(
            src_ref=bufs[which].at[reach_blocks + p],
            dst_ref=bufs[which].at[index],
            send_sem=halo_send.at[which, shifts.index(e), p],
            recv_sem=kv_recv.at[which, index],
            device_id=device(group + e, me),
        )

    routes = [
        (p, [e for e in shifts if 0 <= reach_blocks + p - e * members < blocks])
        for p in range(members)
    ]
    routes.sort(key=lambda route: -len(route[1]))
    def pass_on(which):
        for p, goes in routes:

            @pl.when(me != p)
            def _():
                kv_copy(which, bufs[which].at[0], 0, p, reach_blocks + p).wait_recv()

            for e in goes:

                @pl.when((group + e >= 0) & (group + e < groups))
                def _():
                    halo_copy(which, p, e).start()

    own_v.wait()
    pass_on(0)

    load_q.wait()
    q_copies = []
    for i in range(1, members):
        other = (me + i) % members
        q_rot[i] = rotated(q_in[:, columns(other)], SCORE_SCALE)
        copy = pltpu.make_async_remote_copy(
            src_ref=q_rot.at[i],
            dst_ref=q_buf.at[block(me)],
            send_sem=q_send.at[i],
            recv_sem=q_recv.at[me],
            device_id=device(group, other),
        )
        copy.start()
        q_copies.append(copy)
    q_buf[block(me), :] = rotated(q_in[:, columns(me)], SCORE_SCALE)

    first = (group * members - reach_blocks) * rows
    token = first + lax.broadcasted_iota(jnp.int32, (8, blocks * rows), 1)
    scene = jnp.zeros((8, blocks * rows), jnp.int32)
    load_lengths.wait()
    end = jnp.int32(0)
    for s in range(scenes):
        end = end + lengths_ref[s]
        scene = scene + (token >= end).astype(jnp.int32)
    key_scene[...] = jnp.where(token < 0, -1, scene).astype(jnp.float32)
    for b in range(members):
        row = key_scene[0:1, (reach_blocks + b) * rows : (reach_blocks + b + 1) * rows]
        query_scene[b] = jnp.broadcast_to(row, (128, rows)).T

    pass_on(1)

    def halo_wait():
        for which in range(2):
            for p, goes in routes:
                for e in goes:

                    @pl.when((group - e >= 0) & (group - e < groups))
                    def _():
                        halo_copy(which, p, e).wait_recv()

    lane_head = lax.broadcasted_iota(jnp.int32, (rows, cols), 1) // HD

    own_o = pltpu.make_async_copy(o_buf.at[me], out_ref.at[:, columns(me)], own_sem.at[1])

    def out_copy(other):
        return pltpu.make_async_remote_copy(
            src_ref=o_buf.at[other],
            dst_ref=out_ref.at[:, columns(me)],
            send_sem=o_send.at[other],
            recv_sem=o_recv.at[me],
            device_id=device(group, other),
        )

    free = max(0, members - 2 * reach_blocks)

    def attend(t, carry):
        if isinstance(t, int):
            b = reach_blocks + (me + t) % free
        else:
            turn = (me + t) % (members - free)
            b = turn + free * (turn // reach_blocks)

        @pl.when(b != me)
        def _():
            pltpu.make_async_remote_copy(
                src_ref=q_rot.at[0],
                dst_ref=q_buf.at[block(b)],
                send_sem=q_send.at[0],
                recv_sem=q_recv.at[b],
                device_id=device(group, b),
            ).wait_recv()

        q_tile = q_buf[block(b), :]
        span = pl.ds(pl.multiple_of(b * rows, rows), window)
        count = window // rows
        k_tile = jnp.concatenate([k_buf[b + c] for c in range(count)], axis=1)
        v_tile = v_buf[pl.ds(b, count)].reshape(window, cols)
        q_scene = jnp.concatenate([query_scene[b]] * (window // 128), axis=1)
        bias = jnp.where(q_scene == key_scene[0:1, span], 0.0, NEG_BIG)
        result = jnp.zeros((rows, cols), jnp.float32)
        for h in range(heads):
            q_one = jnp.where(lane_head == h, q_tile, jnp.bfloat16(0.0))
            scores = jnp.dot(q_one, k_tile, preferred_element_type=jnp.float32) + bias
            top = jnp.max(scores, axis=1, keepdims=True)
            weights = jnp.exp(scores - top)
            total = jnp.sum(weights, axis=1, keepdims=True)
            mixed = jnp.dot(
                weights.astype(jnp.bfloat16), v_tile, preferred_element_type=jnp.float32
            )
            result = jnp.where(lane_head == h, mixed / total, result)
        o_buf[b] = result.astype(jnp.bfloat16)

        @pl.when(b != me)
        def _():
            out_copy(b).start()

        @pl.when(b == me)
        def _():
            own_o.start()

        return carry

    for t in range(free):
        attend(t, 0)
    halo_wait()
    lax.fori_loop(0, members - free, attend, 0)

    for copy in v_copies + k_copies + q_copies:
        copy.wait_send()
    for which in range(2):
        for p, goes in routes:
            for e in goes:

                @pl.when((group + e >= 0) & (group + e < groups))
                def _():
                    halo_copy(which, p, e).wait_send()

    for i in range(1, members):
        out_copy((me + i) % members).wait_send()
    for i in range(1, members):
        other = (me + i) % members
        pltpu.make_async_remote_copy(
            src_ref=o_buf.at[0],
            dst_ref=out_ref.at[:, columns(other)],
            send_sem=o_send.at[0],
            recv_sem=o_recv.at[other],
            device_id=device(group, other),
        ).wait_recv()
    own_o.wait()


def local(queries, keys, values, coords, lengths):
    rows, all_cols = queries.shape
    head_count = lax.axis_size("head")
    seq_count = lax.axis_size("seq")
    members = GROUP_DEVICES
    groups = seq_count * head_count // members
    cols = all_cols // members
    scenes = lengths.shape[0]
    total = rows * seq_count * head_count
    longest = 3 * total // scenes
    reach_blocks = -(-(longest - 1) // rows)
    blocks = members + 2 * reach_blocks
    spans = -(-reach_blocks // members)
    sizes = (head_count, members, groups, rows, cols, reach_blocks, scenes)
    window = (2 * reach_blocks + 1) * rows
    bf16, dma = jnp.bfloat16, pltpu.SemaphoreType.DMA
    in_hbm = pl.BlockSpec(memory_space=pltpu.HBM)
    return pl.pallas_call(
        functools.partial(attention_kernel, sizes),
        out_shape=jax.ShapeDtypeStruct((rows, all_cols), bf16),
        in_specs=[in_hbm] * 5,
        out_specs=in_hbm,
        scratch_shapes=[
            pltpu.VMEM(coords.shape, jnp.int32),
            pltpu.SMEM(lengths.shape, jnp.int32),
            pltpu.VMEM((rows, all_cols), bf16),
            pltpu.VMEM((rows, all_cols), bf16),
            pltpu.VMEM((members, rows, cols), bf16),
            pltpu.VMEM((members, cols, rows), bf16),
            pltpu.VMEM((members * rows, cols), bf16),
            pltpu.VMEM((blocks, cols, rows), bf16),
            pltpu.VMEM((blocks, rows, cols), bf16),
            pltpu.VMEM((members, rows, cols), bf16),
            pltpu.VMEM((8, blocks * rows), jnp.float32),
            pltpu.VMEM((members, rows, 128), jnp.float32),
            dma((4,)),
            dma((members,)),
            dma((members,)),
            dma((2, members)),
            dma((2, blocks)),
            dma((2, 2 * spans, members)),
            dma((members,)),
            dma((members,)),
            dma((2,)),
        ],
        compiler_params=pltpu.CompilerParams(
            collective_id=0, has_side_effects=True, vmem_limit_bytes=63 * 1024 * 1024
        ),
        cost_estimate=pl.CostEstimate(
            flops=4 * members * rows * window * cols,
            bytes_accessed=8 * rows * all_cols,
            transcendentals=members * rows * window * (cols // HD),
        ),
    )(queries, keys, values, coords, lengths)


def solution(mesh):
    in_specs = (
        P(("dp", "seq", "head"), None),
        P(("dp", "seq", "head"), None),
        P(("dp", "seq", "head"), None),
        P(None, ("dp", "seq", "head")),
        P("dp"),
    )
    out_specs = P(("dp", "seq", "head"), None)
    return jax.shard_map(local, mesh=mesh, in_specs=in_specs, out_specs=out_specs, check_vma=False)
```

time: 47.2 us -> 38.9 us (0.82)
  Pallas kernels: 40.9 us -> 36.8 us
  local copies, waits for them, and re-layouts: 5.97 us -> 1.88 us
    unnamed x13 -> x1, local copies, waits for them, and re-layouts: 5.97 us -> 1.88 us
    pallas_call x1, Pallas kernels: 40.9 us -> 36.8 us  [local(): pl.pallas_call(functools.partial(attention_kernel, sizes), out_shape=jax....]
where the time goes in v1:
time: 38.9 us; the launch traced here: 38.7 us
  Pallas kernels  36.8 us (95%)
  local copies, waits for them, and re-layouts  1.88 us (5%)
    pallas_call x1, Pallas kernels, local(): pl.pallas_call(functools.partial(attention_kernel, sizes), out_shape=jax....  36.8 us
    unnamed x1, local copies, waits for them, and re-layouts  1.88 us

profile of v1, /device:TPU:0, one launch (start us, length us, event | category | flops | bytes accessed | tf_op | source)
XLA Modules:
  0.0 38.7 jit_solution(18400342095835597638)
XLA Ops:
  0.0 36.8 %shard_map.55 = bf16[128,2048]{1,0:T(8,128)(2,1)} custom-call(bf16[128,2048]{1,0:T(8,128)(2,1)} %q_hbm.1, bf16[128,2048]{1,0:T(8,128)(2,1)} %k_hbm.1, bf16[128,2048]{1,0:T(8,128)(2,1)} %v_hbm.1, s32[3,128]{1,0:T(4,128)} %coords_hbm.1, s32[32]{0:T(128)} %lengths_hbm.1), custom_call_target="tpu_custom_call" | custom-call | flops 939524096 | bytes 2097152 | tf_op jit(solution)/shard_map/pallas_call | solution.py:328
  36.9 1.9 %copy.7 = bf16[128,2048]{1,0:T(8,128)(2,1)} copy(bf16[128,2048]{1,0:T(8,128)(2,1)} %shard_map.55) | data formatting | bytes 1048576

commit v2 on v1

v2 whole, which is shorter than its diff:
```python
import functools

import jax
import jax.numpy as jnp
import numpy as np
from jax import lax
from jax.experimental import pallas as pl
from jax.experimental.pallas import tpu as pltpu
from jax.sharding import PartitionSpec as P

HD = 64
GROUP_DEVICES = 8
PARTS = 1
WAVES = 1
NEG_BIG = -1e30
SCORE_SCALE = 0.125


def frequencies():
    pair_count = HD // 2
    exponent = (3 * np.arange(pair_count) % pair_count) / pair_count
    return [float(f) for f in (100.0 ** -exponent).astype(np.float32)]


def attention_kernel(
    sizes,
    q_hbm, k_hbm, v_hbm, coords_hbm, lengths_hbm,
    out_ref,
    coords_ref, lengths_ref, q_in, k_in, q_rot, k_rot, q_buf, k_buf, v_buf, o_buf,
    key_scene, query_scene,
    in_sem, q_send, q_recv, kv_send, kv_recv, halo_send, o_send, o_recv, own_v_sem, own_o_sem,
):
    head_count, members, groups, rows, cols, parts, reach_blocks, scenes = sizes
    heads = cols // HD
    spans = -(-reach_blocks // members)
    blocks = members + 2 * reach_blocks
    count = 2 * reach_blocks + 1
    window = count * rows
    flat = lax.axis_index("seq") * head_count + lax.axis_index("head")
    group = flat // members
    me = flat % members

    def device(group_at, member_at):
        at = group_at * members + member_at
        return {"seq": at // head_count, "head": at % head_count}

    def columns(member_at, part):
        return pl.ds(pl.multiple_of((member_at * parts + part) * cols, cols), cols)

    shifts = [e for d in range(1, spans + 1) for e in (d, -d)]
    others = [(i, (me + i) % members) for i in range(1, members)]

    load_k = pltpu.make_async_copy(k_hbm, k_in, in_sem.at[0])
    load_q = pltpu.make_async_copy(q_hbm, q_in, in_sem.at[1])
    load_coords = pltpu.make_async_copy(coords_hbm, coords_ref, in_sem.at[2])
    load_lengths = pltpu.make_async_copy(lengths_hbm, lengths_ref, in_sem.at[3])
    load_coords.start()
    load_k.start()
    load_q.start()
    load_lengths.start()
    own_v = [
        pltpu.make_async_copy(
            v_hbm.at[:, columns(me, part)], v_buf.at[part, reach_blocks + me], own_v_sem.at[part]
        )
        for part in range(parts)
    ]
    for copy in own_v:
        copy.start()

    barrier = pltpu.get_barrier_semaphore()
    for i, other in others:
        pl.semaphore_signal(barrier, inc=1, device_id=device(group, other))
    expected = members - 1
    for e in shifts:
        there = (group + e >= 0) & (group + e < groups)

        @pl.when(there)
        def _():
            pl.semaphore_signal(barrier, inc=1, device_id=device(group + e, me))

        expected = expected + there.astype(jnp.int32)
    pl.semaphore_wait(barrier, expected)

    bufs = (v_buf, k_buf)

    def kv_copy(which, part, source, i, other, index):
        return pltpu.make_async_remote_copy(
            src_ref=source,
            dst_ref=bufs[which].at[part, index],
            send_sem=kv_send.at[which, part, i],
            recv_sem=kv_recv.at[which, part, index],
            device_id=device(group, other),
        )

    def v_copy(part, i, other):
        source = v_hbm.at[:, columns(other, part)]
        return kv_copy(0, part, source, i, other, reach_blocks + me)

    def k_copy(part, i, other):
        return kv_copy(1, part, k_rot.at[part, i], i, other, reach_blocks + me)

    wave_rows = rows // WAVES

    def q_copy(part, wave, i, other, at):
        cut = slice(wave * wave_rows, (wave + 1) * wave_rows)
        return pltpu.make_async_remote_copy(
            src_ref=q_rot.at[part, i, cut],
            dst_ref=q_buf.at[part, at, cut],
            send_sem=q_send.at[part, wave, i],
            recv_sem=q_recv.at[part, wave, at],
            device_id=device(group, other),
        )

    def start_v(part):
        for i, other in others:
            v_copy(part, i, other).start()

    start_v(0)

    pair = lax.broadcasted_iota(jnp.int32, (HD // 2, rows), 0)
    axis_of = 3 * pair // (HD // 2)
    load_coords.wait()
    position = jnp.where(
        axis_of == 0,
        coords_ref[0:1, :],
        jnp.where(axis_of == 1, coords_ref[1:2, :], coords_ref[2:3, :]),
    ).astype(jnp.float32)
    frequency = jnp.zeros((HD // 2, rows), jnp.float32)
    for p, value in enumerate(frequencies()):
        frequency = jnp.where(pair == p, value, frequency)
    angles = position * frequency

    def spread(table):
        return jnp.concatenate([table] * (cols // (HD // 2)), axis=0).T

    cos_all = spread(jnp.cos(angles))
    sin_all = spread(jnp.sin(angles))
    from_row = lax.broadcasted_iota(jnp.int32, (cols, cols), 0)
    to_col = lax.broadcasted_iota(jnp.int32, (cols, cols), 1)
    front = to_col % HD < HD // 2
    swap = jnp.where(
        front & (from_row == to_col + HD // 2),
        -1.0,
        jnp.where((to_col % HD >= HD // 2) & (from_row == to_col - HD // 2), 1.0, 0.0),
    ).astype(jnp.bfloat16)

    def rotated(tile, scale):
        swapped = jnp.dot(tile, swap, preferred_element_type=jnp.float32)
        turned = tile.astype(jnp.float32) * cos_all + swapped * sin_all
        return (turned * scale).astype(jnp.bfloat16)

    def rotate_k(part, send):
        for i, other in others:
            k_rot[part, i] = rotated(k_in[:, columns(other, part)], 1.0).T
            if send:
                k_copy(part, i, other).start()
        k_buf[part, reach_blocks + me] = rotated(k_in[:, columns(me, part)], 1.0).T

    def rotate_q(part, send):
        for i, other in others:
            q_rot[part, i] = rotated(q_in[:, columns(other, part)], SCORE_SCALE)
            if send:
                q_copy(part, 0, i, other, me).start()
        q_buf[part, me] = rotated(q_in[:, columns(me, part)], SCORE_SCALE)
        for wave in range(1, WAVES):
            for i, other in others:
                q_copy(part, wave, i, other, me).start()

    load_k.wait()
    rotate_k(0, True)
    load_q.wait()
    rotate_q(0, True)

    for e in shifts:
        held = [p for p in range(members) if 0 <= reach_blocks + p - e * members < blocks]
        low = reach_blocks + held[0] - e * members
        high = reach_blocks + held[-1] - e * members + 1

        @pl.when((group - e < 0) | (group - e >= groups))
        def _():
            for buf in bufs:
                for part in range(parts):
                    buf[part, low:high] = jnp.zeros((high - low,) + buf.shape[2:], jnp.bfloat16)

    def halo_copy(which, part, p, e):
        index = reach_blocks + p - e * members
        return pltpu.make_async_remote_copy(
            src_ref=bufs[which].at[part, reach_blocks + p],
            dst_ref=bufs[which].at[part, index],
            send_sem=halo_send.at[which, part, shifts.index(e), p],
            recv_sem=kv_recv.at[which, part, index],
            device_id=device(group + e, me),
        )

    routes = [
        (p, [e for e in shifts if 0 <= reach_blocks + p - e * members < blocks])
        for p in range(members)
    ]
    routes.sort(key=lambda route: -len(route[1]))

    def pass_on(which, part):
        for p, goes in routes:

            @pl.when(me != p)
            def _():
                kv_copy(which, part, bufs[which].at[part, 0], 0, p, reach_blocks + p).wait_recv()

            for e in goes:

                @pl.when((group + e >= 0) & (group + e < groups))
                def _():
                    halo_copy(which, part, p, e).start()

    def halo_wait(part):
        for which in range(2):
            for p, goes in routes:
                for e in goes:

                    @pl.when((group - e >= 0) & (group - e < groups))
                    def _():
                        halo_copy(which, part, p, e).wait_recv()

    lane_head = lax.broadcasted_iota(jnp.int32, (wave_rows, cols), 1) // HD

    def own_o(part):
        return pltpu.make_async_copy(
            o_buf.at[part, me], out_ref.at[:, columns(me, part)], own_o_sem.at[part]
        )

    def out_copy(part, wave, other, writer):
        cut = slice(wave * wave_rows, (wave + 1) * wave_rows)
        return pltpu.make_async_remote_copy(
            src_ref=o_buf.at[part, other, cut],
            dst_ref=out_ref.at[cut, columns(writer, part)],
            send_sem=o_send.at[part, wave, other],
            recv_sem=o_recv.at[part, wave, writer],
            device_id=device(group, other),
        )

    free = max(0, members - 2 * reach_blocks)

    def mixed_rows(part, wave, b):
        cut = slice(wave * wave_rows, (wave + 1) * wave_rows)
        q_tile = q_buf[part, b, cut]
        span = pl.ds(pl.multiple_of(b * rows, rows), window)
        k_tile = jnp.concatenate([k_buf[part, b + c] for c in range(count)], axis=1)
        v_tile = v_buf[part, pl.ds(b, count)].reshape(window, cols)
        q_scene = jnp.concatenate([query_scene[b, cut]] * (window // 128), axis=1)
        bias = jnp.where(q_scene == key_scene[0:1, span], 0.0, NEG_BIG)
        result = jnp.zeros((wave_rows, cols), jnp.float32)
        for h in range(heads):
            q_one = jnp.where(lane_head == h, q_tile, jnp.bfloat16(0.0))
            scores = jnp.dot(q_one, k_tile, preferred_element_type=jnp.float32) + bias
            top = jnp.max(scores, axis=1, keepdims=True)
            weights = jnp.exp(scores - top)
            total = jnp.sum(weights, axis=1, keepdims=True)
            mixed = jnp.dot(
                weights.astype(jnp.bfloat16), v_tile, preferred_element_type=jnp.float32
            )
            result = jnp.where(lane_head == h, mixed / total, result)
        return result.astype(jnp.bfloat16)

    def attend(part, wave, picked):
        cut = slice(wave * wave_rows, (wave + 1) * wave_rows)
        for b in picked:

            @pl.when(b != me)
            def _():
                q_copy(part, wave, 0, b, b).wait_recv()

        results = [mixed_rows(part, wave, b) for b in picked]
        for b, result in zip(picked, results):
            o_buf[part, b, cut] = result
        for b in picked:

            @pl.when(b != me)
            def _():
                out_copy(part, wave, b, me).start()

    def later(t):
        turn = (me + t) % (members - free)
        return turn + free * (turn // reach_blocks)

    def attend_all(part):
        for wave in range(WAVES):
            for t in range(0, free, 2):
                attend(part, wave, [reach_blocks + (me + t + u) % free for u in range(2)])
            if wave == 0:
                halo_wait(part)

            @pl.loop(0, (members - free) // 2)
            def _(t):
                attend(part, wave, [later(2 * t), later(2 * t + 1)])

        own_o(part).start()

    own_v[0].wait()
    pass_on(0, 0)
    for part in range(1, parts):
        start_v(part)
        rotate_k(part, True)

    first = (group * members - reach_blocks) * rows
    token = first + lax.broadcasted_iota(jnp.int32, (8, blocks * rows), 1)
    scene = jnp.zeros((8, blocks * rows), jnp.int32)
    load_lengths.wait()
    end = jnp.int32(0)
    for s in range(scenes):
        end = end + lengths_ref[s]
        scene = scene + (token >= end).astype(jnp.int32)
    key_scene[...] = jnp.where(token < 0, -1, scene).astype(jnp.float32)
    for b in range(members):
        row = key_scene[0:1, (reach_blocks + b) * rows : (reach_blocks + b + 1) * rows]
        query_scene[b] = jnp.broadcast_to(row, (128, rows)).T

    pass_on(1, 0)
    for part in range(1, parts):
        rotate_q(part, True)

    for part in range(parts):
        if part:
            own_v[part].wait()
            pass_on(0, part)
            pass_on(1, part)
        attend_all(part)

    for part in range(parts):
        for i, other in others:
            v_copy(part, i, other).wait_send()
            k_copy(part, i, other).wait_send()
            for wave in range(WAVES):
                q_copy(part, wave, i, other, me).wait_send()
        for which in range(2):
            for p, goes in routes:
                for e in goes:

                    @pl.when((group + e >= 0) & (group + e < groups))
                    def _():
                        halo_copy(which, part, p, e).wait_send()

        for wave in range(WAVES):
            for i, other in others:
                out_copy(part, wave, other, me).wait_send()
            for i, other in others:
                out_copy(part, wave, other, other).wait_recv()
        own_o(part).wait()


def local(queries, keys, values, coords, lengths):
    rows, all_cols = queries.shape
    head_count = lax.axis_size("head")
    seq_count = lax.axis_size("seq")
    members = GROUP_DEVICES
    groups = seq_count * head_count // members
    parts = PARTS
    cols = all_cols // members // parts
    scenes = lengths.shape[0]
    total = rows * seq_count * head_count
    longest = 3 * total // scenes
    reach_blocks = -(-(longest - 1) // rows)
    blocks = members + 2 * reach_blocks
    spans = -(-reach_blocks // members)
    sizes = (head_count, members, groups, rows, cols, parts, reach_blocks, scenes)
    window = (2 * reach_blocks + 1) * rows
    bf16, dma = jnp.bfloat16, pltpu.SemaphoreType.DMA
    in_hbm = pl.BlockSpec(memory_space=pltpu.HBM)
    return pl.pallas_call(
        functools.partial(attention_kernel, sizes),
        out_shape=jax.ShapeDtypeStruct((rows, all_cols), bf16),
        in_specs=[in_hbm] * 5,
        out_specs=in_hbm,
        scratch_shapes=[
            pltpu.VMEM(coords.shape, jnp.int32),
            pltpu.SMEM(lengths.shape, jnp.int32),
            pltpu.VMEM((rows, all_cols), bf16),
            pltpu.VMEM((rows, all_cols), bf16),
            pltpu.VMEM((parts, members, rows, cols), bf16),
            pltpu.VMEM((parts, members, cols, rows), bf16),
            pltpu.VMEM((parts, members, rows, cols), bf16),
            pltpu.VMEM((parts, blocks, cols, rows), bf16),
            pltpu.VMEM((parts, blocks, rows, cols), bf16),
            pltpu.VMEM((parts, members, rows, cols), bf16),
            pltpu.VMEM((8, blocks * rows), jnp.float32),
            pltpu.VMEM((members, rows, 128), jnp.float32),
            dma((4,)),
            dma((parts, WAVES, members)),
            dma((parts, WAVES, members)),
            dma((2, parts, members)),
            dma((2, parts, blocks)),
            dma((2, parts, 2 * spans, members)),
            dma((parts, WAVES, members)),
            dma((parts, WAVES, members)),
            dma((parts,)),
            dma((parts,)),
        ],
        compiler_params=pltpu.CompilerParams(
            collective_id=0, has_side_effects=True, vmem_limit_bytes=63 * 1024 * 1024
        ),
        cost_estimate=pl.CostEstimate(
            flops=4 * members * rows * window * cols * parts,
            bytes_accessed=8 * rows * all_cols,
            transcendentals=members * rows * window * (cols // HD) * parts,
        ),
    )(queries, keys, values, coords, lengths)


def solution(mesh):
    in_specs = (
        P(("dp", "seq", "head"), None),
        P(("dp", "seq", "head"), None),
        P(("dp", "seq", "head"), None),
        P(None, ("dp", "seq", "head")),
        P("dp"),
    )
    out_specs = P(("dp", "seq", "head"), None)
    return jax.shard_map(local, mesh=mesh, in_specs=in_specs, out_specs=out_specs, check_vma=False)
```

time: 38.9 us -> 37.1 us (0.954)
  Pallas kernels: 36.8 us -> 35 us
    pallas_call x1, Pallas kernels: 36.8 us -> 35 us  [local(): pl.pallas_call(functools.partial(attention_kernel, sizes), out_shape=jax....]
where the time goes in v2:
time: 37.1 us; the launch traced here: 36.9 us
  Pallas kernels  35 us (94%)
  local copies, waits for them, and re-layouts  1.88 us (5%)
    pallas_call x1, Pallas kernels, local(): pl.pallas_call(functools.partial(attention_kernel, sizes), out_shape=jax....  35 us
    unnamed x1, local copies, waits for them, and re-layouts  1.88 us

profile of v2, /device:TPU:0, one launch (start us, length us, event | category | flops | bytes accessed | tf_op | source)
XLA Modules:
  0.0 36.9 jit_solution(331490610302167673)
XLA Ops:
  0.0 35.0 %shard_map.55 = bf16[128,2048]{1,0:T(8,128)(2,1)} custom-call(bf16[128,2048]{1,0:T(8,128)(2,1)} %q_hbm.1, bf16[128,2048]{1,0:T(8,128)(2,1)} %k_hbm.1, bf16[128,2048]{1,0:T(8,128)(2,1)} %v_hbm.1, s32[3,128]{1,0:T(4,128)} %coords_hbm.1, s32[32]{0:T(128)} %lengths_hbm.1), custom_call_target="tpu_custom_call" | custom-call | flops 939524096 | bytes 2097152 | tf_op jit(solution)/shard_map/pallas_call | solution.py:367
  35.0 1.9 %copy.7 = bf16[128,2048]{1,0:T(8,128)(2,1)} copy(bf16[128,2048]{1,0:T(8,128)(2,1)} %shard_map.55) | data formatting | bytes 1048576
